TPU v7x, 256 devices: a whole 4x4x8 slice. The times are simulated.
256 devices in a mesh: lat: 16 (over x_lo, z), lon: 8 (over y, core), section: 2 (over x_hi).
Axes of the slice: x: 4 (x_hi: 2, x_lo: 2; x = x_hi * 2 + x_lo), y: 4, z: 8, core: 2. Of those that a mesh axis runs over, the one named last changes fastest.
Arguments:
- fields: bfloat16 [2, 4, 96, 96, 1024], P(None, None, 'lat', 'lon'), may hold values from -6 to 6
- live_cells: int32 [96, 96], P('lat', 'lon'), may hold values 0 or 1
- norm_gain: bfloat16 [2, 1024], P('section'), may hold values from 0.099609375 to 1.8984375
- q_weight: bfloat16 [2, 1024, 512], P('section'), may hold values from -24 to 24
- k_weight: bfloat16 [2, 1024, 512], P('section'), may hold values from -8 to 8
- v_weight: bfloat16 [2, 1024, 512], P('section'), may hold values from -0.1875 to 0.1875
- o_weight: bfloat16 [2, 512, 1024], P('section'), may hold values from -0.5 to 0.5
- merge_gain: float32 [4096], replicated, may hold values from 0.25 to 1.75
- merge_weight: bfloat16 [4096, 2048], P('lat', 'section'), may hold values from -0.09375 to 0.09375
Outputs:
- merged: bfloat16 [2, 4, 48, 48, 2048], P(None, None, 'lat', 'lon', 'section')
All inputs are finite; a program needn't handle non-finite values. No bound on the sum of `live_cells` on one device may be relied on, other than what follows from the above.
Results may differ from a plain program's by a relative error of at most 0.015.
Values may be sent and summed in bfloat16 or wider, within the bound.
A program may use at most 128 MiB of HBM per device.

v0:
```python
import jax
import jax.numpy as jnp
import numpy as np
from jax import lax
from jax.experimental import pallas as pl
from jax.experimental.pallas import tpu as pltpu
from jax.sharding import PartitionSpec as P

MESH = pl.DeviceIdType.MESH
F32 = jnp.float32
BF16 = jnp.bfloat16
QT = 72
QP = 80
NT = 4 * QP
D = 1024
DH = 512


def tables():
    perm = np.zeros((NT, 384), np.float32)
    share = np.zeros((NT, NT), np.float32)
    phase = np.zeros((384, NT), np.float32)
    cols = np.zeros((4, 128, NT), np.float32)
    rows = np.zeros((4, 8, NT), np.float32)
    where = {}
    for q in range(4):
        for t in range(QT):
            lev, r, c = t // 18, 3 * (q // 2) + t % 18 // 6, 6 * (q % 2) + t % 6
            where[lev, r, c] = q * QP + t
            perm[q * QP + t, (lev * 6 + r) * 16 + c] = 1
            cols[q, c, q * QP + t] = 1
            rows[q, r, q * QP + t] = 1
    for (la, ra, _), a in where.items():
        for (lb, rb, _), b in where.items():
            if la // 2 == lb // 2:
                share[a, b] = 2 if ra // 3 == rb // 3 else 1
    share[np.arange(NT), np.arange(NT)] = 3
    for k in range(4):
        for lev in range(4):
            for a in range(3):
                for b in range(6):
                    phase[k * 96 + (lev * 3 + a) * 8 + b, where[lev, 2 * a + k % 2, 2 * b + k // 2]] = 1
    return perm, share, phase, cols, rows


def kernel(
    x_ref, live_ref, ng_ref, q_ref, k_ref, v_ref, o_ref, mg_ref, mw_ref,
    pm_ref, em_ref, sm_ref, cs_ref, rs_ref,
    out_ref,
    xin, xp, sx, xs, x2h, ar, attb, nrm, qkv, wqkv, ow, oo, wm, pm, em, sm, cs, bias, lvown, lvs, jb, nb,
    lsem, asend, arecv, hsend, hrecv, gsend, grecv, lsend, lrecv, osend, orecv, zsend, zrecv, xsend, xrecv,
    ysend, yrecv, csend, crecv,
):
    i = lax.axis_index("lat")
    j = lax.axis_index("lon")
    s = lax.axis_index("section")
    z = lax.rem(i, 8)
    xl = lax.div(i, 8)
    y = lax.div(j, 2)
    c = lax.rem(j, 2)
    first = s == 0
    second = s == 1
    sign = 2 * s - 1

    def dev(di, dj, sec):
        return (lax.rem(i + di + 16, 16), lax.rem(j + dj + 8, 8), sec)

    def zdev(d):
        return (i - z + lax.rem(z + d + 8, 8), j, s)

    xdev = (lax.rem(i + 8, 16), j, s)
    cdev = (i, j + 1 - 2 * c, s)

    def rc(src, dst, send, recv, device):
        return pltpu.make_async_remote_copy(
            src_ref=src, dst_ref=dst, send_sem=send, recv_sem=recv, device_id=device, device_id_type=MESH
        )

    greet = [dev(0, 1, s), dev(0, -1, s), dev(1, 0, s), dev(-1, 0, s), dev(1, 1, s), dev(-1, -1, s)]
    greet += [dev(0, 2, s), dev(0, -2, s), dev(0, 4, s), zdev(1), zdev(-1), xdev]
    other = 1 - s
    greet += [dev(0, 0, other), dev(0, 1, other), dev(0, -1, other), dev(1, 0, other), dev(-1, 0, other)]
    greet += [dev(1, 1, other), dev(-1, -1, other)]
    barrier = pltpu.get_barrier_semaphore()
    for d in greet:
        pl.semaphore_signal(barrier, inc=1, device_id=d, device_id_type=MESH)

    local = {}
    plan = [
        ("x0", x_ref.at[0], xin.at[0]), ("pm", pm_ref, pm), ("x1", x_ref.at[1], xin.at[1]),
        ("q", q_ref, wqkv.at[:, 0:512]), ("k", k_ref, wqkv.at[:, 512:1024]), ("v", v_ref, wqkv.at[:, 1024:1536]),
        ("cs", cs_ref, cs), ("em", em_ref, em), ("o", o_ref, ow), ("mw", mw_ref, wm.at[xl, z]), ("sm", sm_ref, sm),
    ]
    for n, (name, src, dst) in enumerate(plan):
        local[name] = pltpu.make_async_copy(src, dst, lsem.at[n])
        local[name].start()

    pl.semaphore_wait(barrier, len(greet))

    def oat(ref, piece):
        return ref.at[pl.ds(pl.multiple_of(piece * 64, 64), 64)]

    def piece_at(dj):
        return lax.rem(j + dj + 8, 8)

    o_from = (2, -2, 4)
    sends = []

    def launch(make, *args):
        make(*args).start()
        sends.append((make, args))

    def o_cross():
        return rc(oat(o_ref, j), oat(oo, j), osend.at[0], orecv.at[0], dev(0, 0, other))

    def o_side(n):
        return rc(oat(oo, j), oat(oo, j), osend.at[1 + n], orecv.at[1 + n], dev(0, -o_from[n], s))

    def o_core(n):
        p = oat(oo, piece_at(((0,) + o_from)[n]))
        return rc(p, p, osend.at[4 + n], orecv.at[4 + n], cdev)

    launch(o_cross)

    def o_step1():
        o_cross().wait_recv()
        for n in range(3):
            launch(o_side, n)
        launch(o_core, 0)

    def o_step2():
        for n, dj in enumerate(o_from):
            p = oat(oo, piece_at(dj))
            rc(p, p, osend.at[1 + n], orecv.at[1 + n], dev(0, dj, s)).wait_recv()
            launch(o_core, 1 + n)

    def o_step3():
        for n, dj in enumerate((0,) + o_from):
            p = oat(oo, lax.rem(j + 1 - 2 * c + dj + 8, 8))
            rc(p, p, osend.at[4 + n], orecv.at[4 + n], cdev).wait_recv()

    e = lax.rem(y, 2)
    cls = 2 * e + c
    ocls = 2 * (1 - e) + c

    def rowsof(k, half=None):
        if half is None:
            return pl.ds(pl.multiple_of(k * 64, 64), 64)
        return pl.ds(pl.multiple_of(k * 64 + half * 32, 32), 32)

    def zat(d):
        return lax.rem(z + d + 8, 8)

    def lane_of(chain):
        return xl if chain == 0 else 1 - xl

    def hop_src(chain, way, t):
        d = -way * (t - 1)
        if chain == 0 and t == 1:
            return mw_ref.at[rowsof(cls)]
        return wm.at[lane_of(chain), zat(d), rowsof(cls)]

    def hop_copy(chain, way, t):
        w = 0 if way == 1 else 1
        dst = wm.at[lane_of(chain), zat(-way * (t - 1)), rowsof(cls)]
        return rc(hop_src(chain, way, t), dst, zsend.at[chain, w, t - 1], zrecv.at[chain, w, t - 1], zdev(way))

    def hop(chain, way, t):
        launch(hop_copy, chain, way, t)

    def hop_wait(chain, way, t):
        w = 0 if way == 1 else 1
        dst = wm.at[lane_of(chain), zat(-way * t), rowsof(cls)]
        rc(dst, dst, zsend.at[chain, w, t - 1], zrecv.at[chain, w, t - 1], zdev(way)).wait_recv()

    units = (0, -1, -2, -3, 1, 2, 3, 4)

    def block_at(u, rows):
        if u == 0:
            return wm.at[1 - xl, z, rows]
        return wm.at[:, zat(units[u]), rows]

    def side_copy(u, h):
        ref = block_at(u, rowsof(cls, h))
        return rc(ref, ref, ysend.at[u, h], yrecv.at[u, h], dev(0, 2 - 4 * h, s))

    def core_copy(u, n):
        ref = block_at(u, rowsof(ocls if n else cls))
        return rc(ref, ref, csend.at[u, n], crecv.at[u, n], cdev)

    def spread(u):
        for h in range(2):
            launch(side_copy, u, h)
        launch(core_copy, u, 0)

    def spread2(u):
        for h, dy in ((0, -2), (1, 2)):
            ref = block_at(u, rowsof(ocls, h))
            rc(ref, ref, ysend.at[u, h], yrecv.at[u, h], dev(0, dy, s)).wait_recv()
        launch(core_copy, u, 1)

    def spread3(u):
        for n, k in ((0, 2 * e + 1 - c), (1, 2 * (1 - e) + 1 - c)):
            ref = block_at(u, rowsof(k))
            rc(ref, ref, csend.at[u, n], crecv.at[u, n], cdev).wait_recv()

    def pair_copy():
        return rc(mw_ref.at[rowsof(cls)], wm.at[xl, z, rowsof(cls)], xsend.at[0], xrecv.at[0], xdev)

    def w_p0():
        launch(pair_copy)
        hop(0, 1, 1)
        hop(0, -1, 1)

    def w_p1():
        ref = wm.at[1 - xl, z, rowsof(cls)]
        rc(ref, ref, xsend.at[0], xrecv.at[0], xdev).wait_recv()
        hop(1, 1, 1)
        hop(1, -1, 1)
        spread(0)

    def w_a(t):
        for way in (1, -1):
            hop_wait(0, way, t)
            if t < 3 or way == 1:
                hop(0, way, t + 1)

    def w_b(t):
        for way in (1, -1):
            hop_wait(1, way, t)
            if t < 3 or way == -1:
                hop(1, way, t + 1)
        spread(t)
        spread(3 + t)

    def w_last():
        hop_wait(0, 1, 4)
        hop_wait(1, -1, 4)
        spread(7)

    def permute(m):
        local[f"x{m}"].wait()
        for g in range(24):
            xp[pl.ds(g * 16, 12), :] = xin[m, g]
        if m == 0:
            local["pm"].wait()

        def step(n, carry):
            cols = pl.ds(pl.multiple_of(n * 256, 256), 256)
            got = jnp.dot(pm[...], xp[:, cols], preferred_element_type=F32).astype(BF16)
            sx[m, :, cols] = got

            @pl.when(first)
            def _():
                xs[m, :, cols] = got

            @pl.when(second)
            def _():
                xs[m, pl.ds(3 * QP, QP), cols] = got[3 * QP:, :]

            return carry

        lax.fori_loop(0, 4, step, 0)

    def slot(ref, m, q):
        return ref.at[m, pl.ds(q * QP, QP)]

    def halo(m, q, start):
        up, side = 1 - q // 2, 1 - q % 2
        d = dev(-up, -side, s) if start else dev(up, side, s)
        return rc(slot(sx, m, q), slot(xs, m, q), hsend.at[m, q], hrecv.at[m, q], d)

    def live_copy(q):
        up, side = 1 - q // 2, 1 - q % 2
        return rc(lvown, lvs.at[q], lsend.at[q], lrecv.at[q], dev(-up, -side, s))

    def att_copy(m, q):
        up, side = 1 - q // 2, 1 - q % 2
        return rc(slot(attb, m, q), slot(ar, m, q), asend.at[m, q], arecv.at[m, q], dev(sign * up, sign * side, other))

    def home_copy(m, q):
        up, side = 1 - q // 2, 1 - q % 2
        return rc(slot(xs, m, q), slot(x2h, m, q), gsend.at[m, q], grecv.at[m, q], dev(up, side, s))

    def add_projected(m, src, weight, dst):
        def step(n, carry):
            cols = pl.ds(pl.multiple_of(n * 256, 256), 256)
            got = jnp.dot(src[m], weight[:, cols], preferred_element_type=F32)
            dst[m, :, cols] = (xs[m, :, cols].astype(F32) + got).astype(BF16)
            return carry

        lax.fori_loop(0, 4, step, 0)

    def make_bias():
        local["cs"].wait()
        local["em"].wait()
        alive = jnp.zeros((1, NT), F32)
        for q in range(4):
            got = jnp.dot(lvs[q].astype(BF16), cs[q], preferred_element_type=F32)
            alive += jnp.sum(got * rs_ref[q], axis=0, keepdims=True)
        edge = jnp.where(jnp.logical_and(second, i == 15), 1.5, 0.5)

        def step(n, carry):
            rows = pl.ds(pl.multiple_of(n * 80, 80), 80)
            code = em[rows, :].astype(F32)
            ok = jnp.logical_or(jnp.logical_and(code > edge, alive > 0.5), code > 2.5)
            bias[rows, :] = jnp.where(ok, 0.0, -1e30)
            return carry

        lax.fori_loop(0, 4, step, 0)

    def attend(m):
        def ln(n, carry):
            rows = pl.ds(pl.multiple_of(n * 32, 32), 32)
            v = xs[m, rows, :].astype(F32)
            v = v - jnp.mean(v, axis=-1, keepdims=True)
            var = jnp.mean(v * v, axis=-1, keepdims=True)
            nrm[rows, :] = (v * lax.rsqrt(var + 1e-05) * ng_ref[...].astype(F32)).astype(BF16)
            return carry

        lax.fori_loop(0, 10, ln, 0)
        if m == 0:
            for name in "qkv":
                local[name].wait()

        def project(n, carry):
            cols = pl.ds(pl.multiple_of(n * 256, 256), 256)
            got = jnp.dot(nrm[...], wqkv[:, cols], preferred_element_type=F32)
            qkv[:, cols] = (got * jnp.where(n < 2, 0.125, 1.0)).astype(BF16)
            return carry

        lax.fori_loop(0, 6, project, 0)

        low = lax.broadcasted_iota(jnp.int32, (NT, 128), 1) < 64

        def heads(n, carry):
            base = pl.multiple_of(n * 128, 128)
            qp = qkv[:, pl.ds(base, 128)]
            kp = qkv[:, pl.ds(base + 512, 128)]
            vp = qkv[:, pl.ds(base + 1024, 128)]
            outs = []
            for mask in (low, jnp.logical_not(low)):
                qm = jnp.where(mask, qp, jnp.zeros_like(qp))
                sc = lax.dot_general(qm, kp, (((1,), (1,)), ((), ())), preferred_element_type=F32) + bias[...]
                ex = jnp.exp(sc - jnp.max(sc, axis=-1, keepdims=True))
                total = jnp.sum(ex, axis=-1, keepdims=True)
                got = jnp.dot(ex.astype(BF16), vp, preferred_element_type=F32)
                outs.append(got / total)
            attb[m, :, pl.ds(base, 128)] = jnp.where(low, outs[0], outs[1]).astype(BF16)
            return carry

        lax.fori_loop(0, 4, heads, 0)

    def block(m):
        @pl.when(second)
        def _():
            for q in range(3):
                halo(m, q, False).wait_recv()
            for q in range(4):
                att_copy(m, q).wait_recv()
            add_projected(m, ar, oo, xs)

        attend(m)
        for q in range(4):
            launch(att_copy, m, q)
        if m == 0:
            local["o"].wait()
        add_projected(m, attb, ow, xs)

        @pl.when(second)
        def _():
            for q in range(3):
                home_copy(m, q).start()
            x2h[m, pl.ds(3 * QP, QP), :] = xs[m, pl.ds(3 * QP, QP), :]

    def merge(m):
        def gather(k, carry):
            rows = pl.ds(pl.multiple_of(k * 96, 32), 96)
            jb[k] = jnp.dot(sm[rows, :], x2h[m], preferred_element_type=F32)
            return carry

        lax.fori_loop(0, 4, gather, 0)

        def ln(n, carry):
            rows = pl.ds(pl.multiple_of(n * 16, 16), 16)
            parts = [jb[k, rows, :] for k in range(4)]
            mean = sum(jnp.sum(p, axis=-1, keepdims=True) for p in parts) * (1.0 / 4096)
            parts = [p - mean for p in parts]
            var = sum(jnp.sum(p * p, axis=-1, keepdims=True) for p in parts) * (1.0 / 4096)
            scale = lax.rsqrt(var + 1e-05)
            for k in range(4):
                nb[k, rows, :] = (parts[k] * scale * mg_ref[k]).astype(BF16)
            return carry

        lax.fori_loop(0, 6, ln, 0)

        def out(n, carry):
            cols = pl.ds(pl.multiple_of(n * 256, 256), 256)
            acc = jnp.zeros((96, 256), F32)
            for k in range(4):
                w = wm[k // 2, pl.ds(4 * (k % 2), 4), :, cols].reshape(1024, 256)
                acc += jnp.dot(nb[k], w, preferred_element_type=F32)
            for g in range(12):
                out_ref[m, g, :, cols] = acc[g * 8 : g * 8 + 6].astype(BF16)
            return carry

        lax.fori_loop(0, 4, out, 0)

    w_p0()
    xp[...] = jnp.zeros_like(xp)
    lvown[...] = jnp.zeros_like(lvown)
    lvown[0:6, 0:12] = live_ref[...].astype(F32)

    @pl.when(first)
    def _():
        for q in range(3):
            lvs[q] = lvown[...]

    lvs[3] = lvown[...]

    @pl.when(second)
    def _():
        for q in range(3):
            live_copy(q).start()

    for m in range(2):
        permute(m)

        @pl.when(second)
        def _():
            for q in range(3):
                halo(m, q, True).start()

    @pl.when(second)
    def _():
        for q in range(3):
            live_copy(q).wait_recv()

    make_bias()

    def early():
        w_p1()
        o_step1()
        w_a(1)
        o_step2()
        w_b(1)
        o_step3()

    mark = len(sends)

    @pl.when(second)
    def _():
        early()
        w_a(2)
        w_b(2)

    del sends[mark:]
    block(0)
    block(1)

    mark = len(sends)

    @pl.when(first)
    def _():
        early()
        w_a(2)
        w_b(2)

    w_a(3)
    w_b(3)
    w_last()
    for u in range(8):
        spread2(u)
    local["mw"].wait()
    local["sm"].wait()
    for u in range(8):
        spread3(u)

    for m in range(2):
        @pl.when(first)
        def _():
            for q in range(4):
                att_copy(m, q).wait_recv()
            add_projected(m, ar, oo, x2h)

        @pl.when(second)
        def _():
            for q in range(3):
                home_copy(m, q).wait_recv()

        merge(m)

    for make, args in sends:
        make(*args).wait_send()

    @pl.when(second)
    def _():
        for q in range(3):
            live_copy(q).wait_send()
            for m in range(2):
                halo(m, q, True).wait_send()
                home_copy(m, q).wait_send()


def body(fields, live_cells, norm_gain, q_weight, k_weight, v_weight, o_weight, merge_gain, merge_weight):
    perm, share, phase, cols, rows = tables()
    anywhere = pl.BlockSpec(memory_space=pl.ANY)
    vmem = pl.BlockSpec(memory_space=pltpu.VMEM)
    dma = pltpu.SemaphoreType.DMA
    out = pl.pallas_call(
        kernel,
        out_shape=jax.ShapeDtypeStruct((2, 12, 6, 1024), BF16),
        in_specs=[anywhere, vmem, vmem, anywhere, anywhere, anywhere, anywhere, vmem, anywhere]
        + [anywhere] * 4 + [vmem],
        out_specs=vmem,
        scratch_shapes=[
            pltpu.VMEM((2, 24, 12, D), BF16),
            pltpu.VMEM((384, D), BF16),
            pltpu.VMEM((2, NT, D), BF16),
            pltpu.VMEM((2, NT, D), BF16),
            pltpu.VMEM((2, NT, D), BF16),
            pltpu.VMEM((2, NT, DH), BF16),
            pltpu.VMEM((2, NT, DH), BF16),
            pltpu.VMEM((NT, D), BF16),
            pltpu.VMEM((NT, 3 * DH), BF16),
            pltpu.VMEM((D, 3 * DH), BF16),
            pltpu.VMEM((DH, D), BF16),
            pltpu.VMEM((DH, D), BF16),
            pltpu.VMEM((2, 8, 256, D), BF16),
            pltpu.VMEM((NT, 384), BF16),
            pltpu.VMEM((NT, NT), BF16),
            pltpu.VMEM((384, NT), BF16),
            pltpu.VMEM((4, 128, NT), BF16),
            pltpu.VMEM((NT, NT), F32),
            pltpu.VMEM((8, 128), F32),
            pltpu.VMEM((4, 8, 128), F32),
            pltpu.VMEM((4, 96, D), F32),
            pltpu.VMEM((4, 96, D), BF16),
            dma((11,)),
            dma((2, 4)), dma((2, 4)), dma((2, 4)), dma((2, 4)), dma((2, 4)), dma((2, 4)),
            dma((4,)), dma((4,)), dma((8,)), dma((8,)), dma((2, 2, 4)), dma((2, 2, 4)), dma((1,)), dma((1,)),
            dma((8, 2)), dma((8, 2)), dma((8, 2)), dma((8, 2)),
        ],
        compiler_params=pltpu.CompilerParams(
            collective_id=0, has_side_effects=True, vmem_limit_bytes=52 * 2**20
        ),
    )(
        fields.reshape(2, 24, 12, D),
        live_cells,
        norm_gain,
        q_weight[0],
        k_weight[0],
        v_weight[0],
        o_weight[0],
        merge_gain.reshape(4, 1, D),
        merge_weight,
        jnp.asarray(perm, BF16),
        jnp.asarray(share, BF16),
        jnp.asarray(phase, BF16),
        jnp.asarray(cols, BF16),
        jnp.asarray(rows, F32),
    )
    return out.reshape(2, 4, 3, 6, D)


def solution(mesh):
    placed = (
        P(None, None, "lat", "lon", None),
        P("lat", "lon"),
        P("section", None),
        P("section", None, None),
        P("section", None, None),
        P("section", None, None),
        P("section", None, None),
        P(),
        P("lat", "section"),
    )
    return jax.shard_map(
        body, mesh=mesh, in_specs=placed, out_specs=P(None, None, "lat", "lon", "section"), check_vma=False
    )
```

profile of v0, /device:TPU:5, one launch (start us, length us, event | category | flops | bytes accessed | tf_op | source)
XLA Modules:
  0.0 98.0 jit_solution(14083120424199191306)
XLA Ops:
  0.0 0.0 copy-start.4
  0.0 0.0 copy-start
  0.0 0.0 copy-start.1
  0.0 0.0 copy-start.2
  0.0 0.0 copy-start.3
  0.0 0.0 copy-start.5
  0.0 0.0 copy-start.7
  0.1 0.0 copy-start.6
  0.1 2.9 %copy.15 = bf16[2,4,6,12,1024]{4,3,2,1,0:T(8,128)(2,1)} copy(bf16[2,4,6,12,1024]{4,1,3,2,0:T(4,128)(2,1)} %param.14) | data formatting | bytes 2359296 | tf_op args[0]
  3.0 0.0 copy-done.4
  3.0 0.0 copy-done
  3.0 0.0 copy-done.1
  3.0 0.0 copy-done.2
  3.0 0.0 copy-done.3
  3.0 0.0 copy-done.5
  3.0 0.0 copy-done.7
  3.0 0.0 copy-done.6
  3.0 94.0 %shard_map.136 = bf16[2,12,6,1024]{3,2,1,0:T(8,128)(2,1)S(1)} custom-call(bf16[2,24,12,1024]{3,2,1,0:T(8,128)(2,1)} %bitcast.9, s32[6,12]{1,0:T(8,128)S(1)} %copy-done.6, bf16[1,1024]{1,0:T(2,128)(2,1)S(1)} %copy-done.7, bf16[1024,512]{1,0:T(8,128)(2,1)} %bitcast.10, bf16[1024,512]{1,0:T(8,128)(2,1)} %bitcast.11, bf16[1024,512]{1,0:T(8,128)(2,1)} %bitcast.12, ...), custom_call_target="tpu_custom_call" | custom-call | tf_op jit(solution)/shard_map/pallas_call | solution.py:510
  97.0 0.9 copy.16
Async XLA Ops:
  0.0 3.0 %copy-start.4 = (f32[4,8,320]{2,1,0:T(8,128)S(1)}, f32[4,8,320]{2,1,0:T(8,128)}, u32[]{:S(2)}) copy-start(f32[4,8,320]{2,1,0:T(8,128)} %constant.14.clone.rs_ref) | copy-start | bytes 122884
  0.0 3.0 %copy-start = (bf16[4,128,320]{2,1,0:T(8,128)(2,1)S(1)}, bf16[4,128,320]{2,1,0:T(8,128)(2,1)}, u32[]{:S(2)}) copy-start(bf16[4,128,320]{2,1,0:T(8,128)(2,1)} %constant.13.clone.cs_ref) | copy-start | bytes 983044
  0.0 3.0 %copy-start.1 = (bf16[384,320]{1,0:T(8,128)(2,1)S(1)}, bf16[384,320]{1,0:T(8,128)(2,1)}, u32[]{:S(2)}) copy-start(bf16[384,320]{1,0:T(8,128)(2,1)} %constant.12.clone.sm_ref) | copy-start | bytes 737284
  0.0 3.0 %copy-start.2 = (bf16[320,320]{1,0:T(8,128)(2,1)S(1)}, bf16[320,320]{1,0:T(8,128)(2,1)}, u32[]{:S(2)}) copy-start(bf16[320,320]{1,0:T(8,128)(2,1)} %constant.11.clone.em_ref) | copy-start | bytes 614404
  0.0 3.0 %copy-start.3 = (bf16[320,384]{1,0:T(8,128)(2,1)S(1)}, bf16[320,384]{1,0:T(8,128)(2,1)}, u32[]{:S(2)}) copy-start(bf16[320,384]{1,0:T(8,128)(2,1)} %constant.10.clone.pm_ref) | copy-start | bytes 737284
  0.0 3.0 %copy-start.5 = (f32[4096]{0:T(1024)S(1)}, f32[4096]{0:T(1024)}, u32[]{:S(2)}) copy-start(f32[4096]{0:T(1024)} %param.21) | copy-start | bytes 49156
  0.0 3.0 %copy-start.7 = (bf16[1,1024]{1,0:T(2,128)(2,1)S(1)}, bf16[1,1024]{1,0:T(2,128)(2,1)}, u32[]{:S(2)}) copy-start(bf16[1,1024]{1,0:T(2,128)(2,1)} %ng_ref.1) | copy-start | bytes 6148
  0.1 3.0 %copy-start.6 = (s32[6,12]{1,0:T(8,128)S(1)}, s32[6,12]{1,0:T(8,128)}, u32[]{:S(2)}) copy-start(s32[6,12]{1,0:T(8,128)} %live_ref.1) | copy-start | bytes 868
where the time goes:
time: 98.4 us; the launch traced here: 98 us
  Pallas kernels  94 us (96%)
  local copies, waits for them, and re-layouts  3.9 us (4%)
    pallas_call x1, Pallas kernels, body(): pl.pallas_call(kernel, out_shape=jax.ShapeDtypeStruct((2, 12, 6, 1024), B...  94 us
    unnamed x17, local copies, waits for them, and re-layouts  2.95 us

commit v1 on v0

--- a/solution.py
+++ b/solution.py
@@ -12,34 +12,36 @@
 QT = 72
 QP = 80
 NT = 4 * QP
+HP = 40
+WT = 4 * HP
 D = 1024
 DH = 512
 
 
 def tables():
-    perm = np.zeros((NT, 384), np.float32)
-    share = np.zeros((NT, NT), np.float32)
-    phase = np.zeros((384, NT), np.float32)
-    cols = np.zeros((4, 128, NT), np.float32)
-    rows = np.zeros((4, 8, NT), np.float32)
+    perm = np.zeros((NT, 4 * QT), np.float32)
+    share = np.zeros((WT, WT), np.float32)
+    phase = np.zeros((4 * QP, NT), np.float32)
+    cols = np.zeros((4, 128, WT), np.float32)
+    rows = np.zeros((4, 8, WT), np.float32)
     where = {}
     for q in range(4):
         for t in range(QT):
             lev, r, c = t // 18, 3 * (q // 2) + t % 18 // 6, 6 * (q % 2) + t % 6
-            where[lev, r, c] = q * QP + t
-            perm[q * QP + t, (lev * 6 + r) * 16 + c] = 1
-            cols[q, c, q * QP + t] = 1
-            rows[q, r, q * QP + t] = 1
-    for (la, ra, _), a in where.items():
-        for (lb, rb, _), b in where.items():
-            if la // 2 == lb // 2:
-                share[a, b] = 2 if ra // 3 == rb // 3 else 1
-    share[np.arange(NT), np.arange(NT)] = 3
+            where[lev, r, c] = q * QP + lev // 2 * HP + t % 36
+            perm[where[lev, r, c], (r * 12 + c) * 4 + lev] = 1
+            cols[q, c, q * HP + t % 36] = 1
+            rows[q, r, q * HP + t % 36] = 1
+    for a in range(WT):
+        for b in range(WT):
+            if a % HP < 36 and b % HP < 36:
+                share[a, b] = 2 if a // (2 * HP) == b // (2 * HP) else 1
+    share[np.arange(WT), np.arange(WT)] = 3
     for k in range(4):
         for lev in range(4):
             for a in range(3):
                 for b in range(6):
-                    phase[k * 96 + (lev * 3 + a) * 8 + b, where[lev, 2 * a + k % 2, 2 * b + k // 2]] = 1
+                    phase[k * QP + (a * 6 + b) * 4 + lev, where[lev, 2 * a + k % 2, 2 * b + k // 2]] = 1
     return perm, share, phase, cols, rows
 
 
@@ -88,8 +90,9 @@
     local = {}
     plan = [
         ("x0", x_ref.at[0], xin.at[0]), ("pm", pm_ref, pm), ("x1", x_ref.at[1], xin.at[1]),
+        ("cs", cs_ref, cs), ("em", em_ref, em),
         ("q", q_ref, wqkv.at[:, 0:512]), ("k", k_ref, wqkv.at[:, 512:1024]), ("v", v_ref, wqkv.at[:, 1024:1536]),
-        ("cs", cs_ref, cs), ("em", em_ref, em), ("o", o_ref, ow), ("mw", mw_ref, wm.at[xl, z]), ("sm", sm_ref, sm),
+        ("o", o_ref, ow), ("mw", mw_ref, wm.at[xl, z]), ("sm", sm_ref, sm),
     ]
     for n, (name, src, dst) in enumerate(plan):
         local[name] = pltpu.make_async_copy(src, dst, lsem.at[n])
@@ -238,10 +241,16 @@
         hop_wait(1, -1, 4)
         spread(7)
 
+    def off(m, q):
+        return (1 - q // 2, 1 - q % 2) if m == 0 else (-(q // 2), -(q % 2))
+
+    own = (3, 0)
+    away = ((0, 1, 2), (1, 2, 3))
+
     def permute(m):
         local[f"x{m}"].wait()
-        for g in range(24):
-            xp[pl.ds(g * 16, 12), :] = xin[m, g]
+        for g in range(QT):
+            xp[pl.ds(g * 4, 4), :] = xin[m, g]
         if m == 0:
             local["pm"].wait()
 
@@ -256,7 +265,7 @@
 
             @pl.when(second)
             def _():
-                xs[m, pl.ds(3 * QP, QP), cols] = got[3 * QP:, :]
+                xs[m, pl.ds(own[m] * QP, QP), cols] = got[own[m] * QP : own[m] * QP + QP, :]
 
             return carry
 
@@ -266,20 +275,20 @@
         return ref.at[m, pl.ds(q * QP, QP)]
 
     def halo(m, q, start):
-        up, side = 1 - q // 2, 1 - q % 2
+        up, side = off(m, q)
         d = dev(-up, -side, s) if start else dev(up, side, s)
         return rc(slot(sx, m, q), slot(xs, m, q), hsend.at[m, q], hrecv.at[m, q], d)
 
-    def live_copy(q):
-        up, side = 1 - q // 2, 1 - q % 2
-        return rc(lvown, lvs.at[q], lsend.at[q], lrecv.at[q], dev(-up, -side, s))
+    def live_copy(m, q):
+        up, side = off(m, q)
+        return rc(lvown, lvs.at[m, q], lsend.at[m, q], lrecv.at[m, q], dev(-up, -side, s))
 
     def att_copy(m, q):
-        up, side = 1 - q // 2, 1 - q % 2
+        up, side = off(m, q)
         return rc(slot(attb, m, q), slot(ar, m, q), asend.at[m, q], arecv.at[m, q], dev(sign * up, sign * side, other))
 
     def home_copy(m, q):
-        up, side = 1 - q // 2, 1 - q % 2
+        up, side = off(m, q)
         return rc(slot(xs, m, q), slot(x2h, m, q), gsend.at[m, q], grecv.at[m, q], dev(up, side, s))
 
     def add_projected(m, src, weight, dst):
@@ -291,91 +300,87 @@
 
         lax.fori_loop(0, 4, step, 0)
 
-    def make_bias():
-        local["cs"].wait()
-        local["em"].wait()
-        alive = jnp.zeros((1, NT), F32)
+    def make_bias(m):
+        alive = jnp.zeros((1, WT), F32)
         for q in range(4):
-            got = jnp.dot(lvs[q].astype(BF16), cs[q], preferred_element_type=F32)
+            got = jnp.dot(lvs[m, q].astype(BF16), cs[q], preferred_element_type=F32)
             alive += jnp.sum(got * rs_ref[q], axis=0, keepdims=True)
-        edge = jnp.where(jnp.logical_and(second, i == 15), 1.5, 0.5)
-
-        def step(n, carry):
-            rows = pl.ds(pl.multiple_of(n * 80, 80), 80)
-            code = em[rows, :].astype(F32)
-            ok = jnp.logical_or(jnp.logical_and(code > edge, alive > 0.5), code > 2.5)
-            bias[rows, :] = jnp.where(ok, 0.0, -1e30)
-            return carry
-
-        lax.fori_loop(0, 4, step, 0)
-
-    def attend(m):
-        def ln(n, carry):
-            rows = pl.ds(pl.multiple_of(n * 32, 32), 32)
-            v = xs[m, rows, :].astype(F32)
+        cut = jnp.where(jnp.logical_and(second, i == (15 if m == 0 else 0)), 1.5, 0.5)
+        code = em[...].astype(F32)
+        ok = jnp.logical_or(jnp.logical_and(code > cut, alive > 0.5), code > 2.5)
+        bias[m] = jnp.where(ok, 0.0, -1e30)
+
+    def attend(m, hook):
+        gain = ng_ref[...].astype(F32)
+        for n in range(8):
+            v = xs[m, n * HP : n * HP + HP, :].astype(F32)
             v = v - jnp.mean(v, axis=-1, keepdims=True)
             var = jnp.mean(v * v, axis=-1, keepdims=True)
-            nrm[rows, :] = (v * lax.rsqrt(var + 1e-05) * ng_ref[...].astype(F32)).astype(BF16)
-            return carry
-
-        lax.fori_loop(0, 10, ln, 0)
+            row = n % 2 * WT + n // 2 * HP
+            nrm[row : row + HP, :] = (v * lax.rsqrt(var + 1e-05) * gain).astype(BF16)
         if m == 0:
             for name in "qkv":
                 local[name].wait()
 
         def project(n, carry):
-            cols = pl.ds(pl.multiple_of(n * 256, 256), 256)
+            cols = pl.ds(pl.multiple_of(n * 512, 512), 512)
             got = jnp.dot(nrm[...], wqkv[:, cols], preferred_element_type=F32)
-            qkv[:, cols] = (got * jnp.where(n < 2, 0.125, 1.0)).astype(BF16)
+            qkv[:, cols] = (got * jnp.where(n < 1, 0.125, 1.0)).astype(BF16)
             return carry
 
-        lax.fori_loop(0, 6, project, 0)
-
-        low = lax.broadcasted_iota(jnp.int32, (NT, 128), 1) < 64
+        lax.fori_loop(0, 3, project, 0)
+        hook()
+        low = lax.broadcasted_iota(jnp.int32, (WT, 128), 1) < 64
+        bm = m * s
 
         def heads(n, carry):
             base = pl.multiple_of(n * 128, 128)
-            qp = qkv[:, pl.ds(base, 128)]
-            kp = qkv[:, pl.ds(base + 512, 128)]
-            vp = qkv[:, pl.ds(base + 1024, 128)]
-            outs = []
-            for mask in (low, jnp.logical_not(low)):
-                qm = jnp.where(mask, qp, jnp.zeros_like(qp))
-                sc = lax.dot_general(qm, kp, (((1,), (1,)), ((), ())), preferred_element_type=F32) + bias[...]
-                ex = jnp.exp(sc - jnp.max(sc, axis=-1, keepdims=True))
-                total = jnp.sum(ex, axis=-1, keepdims=True)
-                got = jnp.dot(ex.astype(BF16), vp, preferred_element_type=F32)
-                outs.append(got / total)
-            attb[m, :, pl.ds(base, 128)] = jnp.where(low, outs[0], outs[1]).astype(BF16)
+            for w in range(2):
+                rows = pl.ds(w * WT, WT)
+                qp = qkv[rows, pl.ds(base, 128)]
+                kp = qkv[rows, pl.ds(base + 512, 128)]
+                vp = qkv[rows, pl.ds(base + 1024, 128)]
+                outs = []
+                for mask in (low, jnp.logical_not(low)):
+                    qm = jnp.where(mask, qp, jnp.zeros_like(qp))
+                    sc = lax.dot_general(qm, kp, (((1,), (1,)), ((), ())), preferred_element_type=F32) + bias[bm]
+                    ex = jnp.exp(sc - jnp.max(sc, axis=-1, keepdims=True))
+                    total = jnp.sum(ex, axis=-1, keepdims=True)
+                    got = jnp.dot(ex.astype(BF16), vp, preferred_element_type=F32)
+                    outs.append(got / total)
+                both = jnp.where(low, outs[0], outs[1]).astype(BF16)
+                for q in range(4):
+                    attb[m, pl.ds(q * QP + w * HP, HP), pl.ds(base, 128)] = both[q * HP : q * HP + HP, :]
             return carry
 
         lax.fori_loop(0, 4, heads, 0)
 
-    def block(m):
+    def block(m, middle, after):
         @pl.when(second)
         def _():
-            for q in range(3):
+            for q in away[m]:
                 halo(m, q, False).wait_recv()
             for q in range(4):
                 att_copy(m, q).wait_recv()
             add_projected(m, ar, oo, xs)
 
-        attend(m)
+        attend(m, middle)
         for q in range(4):
             launch(att_copy, m, q)
+        after()
         if m == 0:
             local["o"].wait()
         add_projected(m, attb, ow, xs)
 
         @pl.when(second)
         def _():
-            for q in range(3):
+            for q in away[m]:
                 home_copy(m, q).start()
-            x2h[m, pl.ds(3 * QP, QP), :] = xs[m, pl.ds(3 * QP, QP), :]
+            x2h[m, pl.ds(own[m] * QP, QP), :] = xs[m, pl.ds(own[m] * QP, QP), :]
 
     def merge(m):
         def gather(k, carry):
-            rows = pl.ds(pl.multiple_of(k * 96, 32), 96)
+            rows = pl.ds(pl.multiple_of(k * QP, QP), QP)
             jb[k] = jnp.dot(sm[rows, :], x2h[m], preferred_element_type=F32)
             return carry
 
@@ -392,84 +397,106 @@
                 nb[k, rows, :] = (parts[k] * scale * mg_ref[k]).astype(BF16)
             return carry
 
-        lax.fori_loop(0, 6, ln, 0)
+        lax.fori_loop(0, 5, ln, 0)
 
         def out(n, carry):
             cols = pl.ds(pl.multiple_of(n * 256, 256), 256)
-            acc = jnp.zeros((96, 256), F32)
+            acc = jnp.zeros((QP, 256), F32)
             for k in range(4):
                 w = wm[k // 2, pl.ds(4 * (k % 2), 4), :, cols].reshape(1024, 256)
                 acc += jnp.dot(nb[k], w, preferred_element_type=F32)
-            for g in range(12):
-                out_ref[m, g, :, cols] = acc[g * 8 : g * 8 + 6].astype(BF16)
+            for g in range(18):
+                out_ref[m, g, :, cols] = acc[g * 4 : g * 4 + 4].astype(BF16)
             return carry
 
         lax.fori_loop(0, 4, out, 0)
 
-    w_p0()
-    xp[...] = jnp.zeros_like(xp)
     lvown[...] = jnp.zeros_like(lvown)
     lvown[0:6, 0:12] = live_ref[...].astype(F32)
 
     @pl.when(first)
     def _():
-        for q in range(3):
-            lvs[q] = lvown[...]
-
-    lvs[3] = lvown[...]
+        w_p0()
+        for m in range(2):
+            for q in away[m]:
+                lvs[m, q] = lvown[...]
+
+    for m in range(2):
+        lvs[m, own[m]] = lvown[...]
 
     @pl.when(second)
     def _():
-        for q in range(3):
-            live_copy(q).start()
-
-    for m in range(2):
-        permute(m)
-
-        @pl.when(second)
-        def _():
-            for q in range(3):
-                halo(m, q, True).start()
+        for m in range(2):
+            for q in away[m]:
+                live_copy(m, q).start()
+
+    permute(0)
 
     @pl.when(second)
     def _():
-        for q in range(3):
-            live_copy(q).wait_recv()
-
-    make_bias()
-
-    def early():
-        w_p1()
-        o_step1()
-        w_a(1)
-        o_step2()
-        w_b(1)
-        o_step3()
-
-    mark = len(sends)
-
-    @pl.when(second)
-    def _():
-        early()
-        w_a(2)
-        w_b(2)
-
-    del sends[mark:]
-    block(0)
-    block(1)
-
-    mark = len(sends)
-
-    @pl.when(first)
-    def _():
-        early()
-        w_a(2)
-        w_b(2)
-
-    w_a(3)
-    w_b(3)
+        for q in away[0]:
+            halo(0, q, True).start()
+        permute(1)
+        for q in away[1]:
+            halo(1, q, True).start()
+        w_p0()
+        for m in range(2):
+            for q in away[m]:
+                live_copy(m, q).wait_recv()
+
+    del sends[1:]
+    local["cs"].wait()
+    local["em"].wait()
+    make_bias(0)
+
+    def only(which, *steps):
+        def run():
+            mark = len(sends)
+
+            @pl.when(which)
+            def _():
+                for f, *args in steps:
+                    f(*args)
+
+            pending.extend(sends[mark:])
+            del sends[mark:]
+
+        return run
+
+    pending = []
+
+    def remake():
+        sends.append((pair_copy, ()))
+        for way in (1, -1):
+            for chain in range(2):
+                for n in range(1, 5 if way == 1 - 2 * chain else 4):
+                    sends.append((hop_copy, (chain, way, n)))
+        for n in range(3):
+            sends.append((o_side, (n,)))
+        for n in range(4):
+            sends.append((o_core, (n,)))
+        for u in range(7):
+            for h in range(2):
+                sends.append((side_copy, (u, h)))
+            sends.append((core_copy, (u, 0)))
+        for u in (0, 1, 4, 2, 5):
+            sends.append((core_copy, (u, 1)))
+
+    def both(a, b):
+        def run():
+            only(first, *a)()
+            only(second, *b)()
+
+        return run
+
+    only(second, (make_bias, 1), (o_step1,), (w_p1,), (o_step2,), (w_a, 1), (o_step3,), (w_b, 1), (spread2, 0))()
+    block(0, both([(w_p1,)], [(w_a, 2)]), both([(w_a, 1), (permute, 1)], [(w_b, 2), (spread2, 1), (spread2, 4)]))
+    block(1, both([(w_b, 1)], [(w_a, 3)]), both([(w_a, 2), (o_step1,)], [(w_b, 3), (spread2, 2), (spread2, 5)]))
+    only(first, (w_b, 2), (o_step2,), (spread2, 0), (spread2, 1), (spread2, 4), (w_a, 3), (spread2, 2), (spread2, 5), (w_b, 3), (o_step3,))()
+    del pending[:]
+    remake()
     w_last()
-    for u in range(8):
+    for u in (3, 6, 7):
         spread2(u)
     local["mw"].wait()
     local["sm"].wait()
@@ -485,7 +512,7 @@
 
         @pl.when(second)
         def _():
-            for q in range(3):
+            for q in away[m]:
                 home_copy(m, q).wait_recv()
 
         merge(m)
@@ -495,27 +522,27 @@
 
     @pl.when(second)
     def _():
-        for q in range(3):
-            live_copy(q).wait_send()
-            for m in range(2):
+        for m in range(2):
+            for q in away[m]:
+                live_copy(m, q).wait_send()
                 halo(m, q, True).wait_send()
                 home_copy(m, q).wait_send()
 
 
 def body(fields, live_cells, norm_gain, q_weight, k_weight, v_weight, o_weight, merge_gain, merge_weight):
     perm, share, phase, cols, rows = tables()
-    anywhere = pl.BlockSpec(memory_space=pl.ANY)
+    anywhere = pl.BlockSpec(memory_space=pltpu.HBM)
     vmem = pl.BlockSpec(memory_space=pltpu.VMEM)
     dma = pltpu.SemaphoreType.DMA
     out = pl.pallas_call(
         kernel,
-        out_shape=jax.ShapeDtypeStruct((2, 12, 6, 1024), BF16),
+        out_shape=jax.ShapeDtypeStruct((2, 18, 4, 1024), BF16),
         in_specs=[anywhere, vmem, vmem, anywhere, anywhere, anywhere, anywhere, vmem, anywhere]
         + [anywhere] * 4 + [vmem],
         out_specs=vmem,
         scratch_shapes=[
-            pltpu.VMEM((2, 24, 12, D), BF16),
-            pltpu.VMEM((384, D), BF16),
+            pltpu.VMEM((2, QT, 4, D), BF16),
+            pltpu.VMEM((4 * QT, D), BF16),
             pltpu.VMEM((2, NT, D), BF16),
             pltpu.VMEM((2, NT, D), BF16),
             pltpu.VMEM((2, NT, D), BF16),
@@ -527,25 +554,25 @@
             pltpu.VMEM((DH, D), BF16),
             pltpu.VMEM((DH, D), BF16),
             pltpu.VMEM((2, 8, 256, D), BF16),
-            pltpu.VMEM((NT, 384), BF16),
-            pltpu.VMEM((NT, NT), BF16),
-            pltpu.VMEM((384, NT), BF16),
-            pltpu.VMEM((4, 128, NT), BF16),
-            pltpu.VMEM((NT, NT), F32),
+            pltpu.VMEM((NT, 4 * QT), BF16),
+            pltpu.VMEM((WT, WT), BF16),
+            pltpu.VMEM((4 * QP, NT), BF16),
+            pltpu.VMEM((4, 128, WT), BF16),
+            pltpu.VMEM((2, WT, WT), F32),
             pltpu.VMEM((8, 128), F32),
-            pltpu.VMEM((4, 8, 128), F32),
-            pltpu.VMEM((4, 96, D), F32),
-            pltpu.VMEM((4, 96, D), BF16),
+            pltpu.VMEM((2, 4, 8, 128), F32),
+            pltpu.VMEM((4, QP, D), F32),
+            pltpu.VMEM((4, QP, D), BF16),
             dma((11,)),
             dma((2, 4)), dma((2, 4)), dma((2, 4)), dma((2, 4)), dma((2, 4)), dma((2, 4)),
-            dma((4,)), dma((4,)), dma((8,)), dma((8,)), dma((2, 2, 4)), dma((2, 2, 4)), dma((1,)), dma((1,)),
+            dma((2, 4)), dma((2, 4)), dma((8,)), dma((8,)), dma((2, 2, 4)), dma((2, 2, 4)), dma((1,)), dma((1,)),
             dma((8, 2)), dma((8, 2)), dma((8, 2)), dma((8, 2)),
         ],
         compiler_params=pltpu.CompilerParams(
             collective_id=0, has_side_effects=True, vmem_limit_bytes=52 * 2**20
         ),
     )(
-        fields.reshape(2, 24, 12, D),
+        fields.transpose(0, 2, 3, 1, 4).reshape(2, QT, 4, D),
         live_cells,
         norm_gain,
         q_weight[0],
@@ -560,7 +587,7 @@
         jnp.asarray(cols, BF16),
         jnp.asarray(rows, F32),
     )
-    return out.reshape(2, 4, 3, 6, D)
+    return out.reshape(2, 3, 6, 4, D).transpose(0, 3, 1, 2, 4)
 
 
 def solution(mesh):

time: 98.4 us -> 79.2 us (0.80)
  Pallas kernels: 94 us -> 70 us
  local copies, waits for them, and re-layouts: 3.9 us -> 8.33 us
    pallas_call x1, Pallas kernels: 94 us -> 70 us  [body(): pl.pallas_call(kernel, out_shape=jax.ShapeDtypeStruct((2, 18, 4, 1024), B...]
    unnamed x17 -> x19, local copies, waits for them, and re-layouts: 2.95 us -> 8.33 us
where the time goes in v1:
time: 79.2 us; the launch traced here: 78.3 us
  Pallas kernels  70 us (88%)
  local copies, waits for them, and re-layouts  8.33 us (11%)
    pallas_call x1, Pallas kernels, body(): pl.pallas_call(kernel, out_shape=jax.ShapeDtypeStruct((2, 18, 4, 1024), B...  70 us
    unnamed x19, local copies, waits for them, and re-layouts  8.33 us

profile of v1, /device:TPU:5, one launch (start us, length us, event | category | flops | bytes accessed | tf_op | source)
XLA Modules:
  0.0 78.3 jit_solution(14654199776613897341)
XLA Ops:
  0.0 0.0 copy-start
  0.0 1.0 %copy-done = bf16[256,1024]{1,0:T(8,128)(2,1)S(1)} copy-done((bf16[256,1024]{1,0:T(8,128)(2,1)S(1)}, bf16[256,1024]{1,0:T(8,128)(2,1)}, u32[]{:S(2)}) %copy-start) | copy-done | bytes 524312
  1.0 0.0 copy-start.1
  1.0 0.9 %copy-done.1 = bf16[4,128,160]{2,1,0:T(8,128)(2,1)S(1)} copy-done((bf16[4,128,160]{2,1,0:T(8,128)(2,1)S(1)}, bf16[4,128,160]{2,1,0:T(8,128)(2,1)}, u32[]{:S(2)}) %copy-start.1) | copy-done | bytes 163864
  2.0 0.0 copy-start.2
  2.0 0.9 %copy-done.2 = bf16[320,320]{1,0:T(8,128)(2,1)S(1)} copy-done((bf16[320,320]{1,0:T(8,128)(2,1)S(1)}, bf16[320,320]{1,0:T(8,128)(2,1)}, u32[]{:S(2)}) %copy-start.2) | copy-done | bytes 204824
  2.9 0.0 copy-start.3
  2.9 0.9 %copy-done.3 = bf16[320,288]{1,0:T(8,128)(2,1)S(1)} copy-done((bf16[320,288]{1,0:T(8,128)(2,1)S(1)}, bf16[320,288]{1,0:T(8,128)(2,1)}, u32[]{:S(2)}) %copy-start.3) | copy-done | bytes 184344
  3.9 0.0 copy-start.4
  3.9 0.9 %copy-done.4 = bf16[160,160]{1,0:T(8,128)(2,1)S(1)} copy-done((bf16[160,160]{1,0:T(8,128)(2,1)S(1)}, bf16[160,160]{1,0:T(8,128)(2,1)}, u32[]{:S(2)}) %copy-start.4) | copy-done | bytes 51224
  4.8 0.0 copy-start.5
  4.8 0.8 copy-done.5
  5.5 0.0 copy-start.6
  5.5 0.7 copy-done.6
  6.2 0.0 copy-start.7
  6.2 0.7 copy-done.7
  6.9 0.0 copy-start.8
  6.9 0.7 copy-done.8
  7.6 70.0 %shard_map.136 = bf16[2,18,4,1024]{3,2,1,0:T(4,128)(2,1)S(1)} custom-call(bf16[2,72,4,1024]{3,2,1,0:T(4,128)(2,1)} %bitcast.13, s32[6,12]{1,0:T(8,128)S(1)} %copy-done.7, bf16[1,1024]{1,0:T(2,128)(2,1)S(1)} %copy-done.8, bf16[1024,512]{1,0:T(8,128)(2,1)} %bitcast.14, bf16[1024,512]{1,0:T(8,128)(2,1)} %bitcast.15, bf16[1024,512]{1,0:T(8,128)(2,1)} %bitcast.16, ...), custom_call_target="tpu_custom_call" | custom-call | tf_op jit(solution)/shard_map/pallas_call | solution.py:537
  77.6 0.7 copy.16
Async XLA Ops:
  0.0 1.0 %copy-start = (bf16[256,1024]{1,0:T(8,128)(2,1)S(1)}, bf16[256,1024]{1,0:T(8,128)(2,1)}, u32[]{:S(2)}) copy-start(bf16[256,1024]{1,0:T(8,128)(2,1)} %mw_ref.1) | copy-start | bytes 1572868
  1.0 0.9 %copy-start.1 = (bf16[4,128,160]{2,1,0:T(8,128)(2,1)S(1)}, bf16[4,128,160]{2,1,0:T(8,128)(2,1)}, u32[]{:S(2)}) copy-start(bf16[4,128,160]{2,1,0:T(8,128)(2,1)} %constant.13.clone.cs_ref) | copy-start | bytes 491524
  2.0 0.9 %copy-start.2 = (bf16[320,320]{1,0:T(8,128)(2,1)S(1)}, bf16[320,320]{1,0:T(8,128)(2,1)}, u32[]{:S(2)}) copy-start(bf16[320,320]{1,0:T(8,128)(2,1)} %constant.12.clone.sm_ref) | copy-start | bytes 614404
  2.9 0.9 %copy-start.3 = (bf16[320,288]{1,0:T(8,128)(2,1)S(1)}, bf16[320,288]{1,0:T(8,128)(2,1)}, u32[]{:S(2)}) copy-start(bf16[320,288]{1,0:T(8,128)(2,1)} %constant.10.clone.pm_ref) | copy-start | bytes 552964
  3.9 0.9 %copy-start.4 = (bf16[160,160]{1,0:T(8,128)(2,1)S(1)}, bf16[160,160]{1,0:T(8,128)(2,1)}, u32[]{:S(2)}) copy-start(bf16[160,160]{1,0:T(8,128)(2,1)} %constant.11.clone.em_ref) | copy-start | bytes 153604
  4.8 0.8 copy-start.5
  5.5 0.7 copy-start.6
  6.2 0.7 copy-start.7
  6.9 0.7 copy-start.8

commit v2 on v1

--- a/solution.py
+++ b/solution.py
@@ -269,7 +269,7 @@
 
             return carry
 
-        lax.fori_loop(0, 4, step, 0)
+        lax.fori_loop(0, 4, step, 0, unroll=True)
 
     def slot(ref, m, q):
         return ref.at[m, pl.ds(q * QP, QP)]
@@ -283,9 +283,13 @@
         up, side = off(m, q)
         return rc(lvown, lvs.at[m, q], lsend.at[m, q], lrecv.at[m, q], dev(-up, -side, s))
 
-    def att_copy(m, q):
+    def att_copy(m, q, h):
         up, side = off(m, q)
-        return rc(slot(attb, m, q), slot(ar, m, q), asend.at[m, q], arecv.at[m, q], dev(sign * up, sign * side, other))
+        rows, cols = pl.ds(q * QP, QP), pl.ds(h * 256, 256)
+        return rc(
+            attb.at[m, rows, cols], ar.at[m, rows, cols], asend.at[m, q, h], arecv.at[m, q, h],
+            dev(sign * up, sign * side, other),
+        )
 
     def home_copy(m, q):
         up, side = off(m, q)
@@ -298,7 +302,7 @@
             dst[m, :, cols] = (xs[m, :, cols].astype(F32) + got).astype(BF16)
             return carry
 
-        lax.fori_loop(0, 4, step, 0)
+        lax.fori_loop(0, 4, step, 0, unroll=True)
 
     def make_bias(m):
         alive = jnp.zeros((1, WT), F32)
@@ -328,7 +332,7 @@
             qkv[:, cols] = (got * jnp.where(n < 1, 0.125, 1.0)).astype(BF16)
             return carry
 
-        lax.fori_loop(0, 3, project, 0)
+        lax.fori_loop(0, 3, project, 0, unroll=True)
         hook()
         low = lax.broadcasted_iota(jnp.int32, (WT, 128), 1) < 64
         bm = m * s
@@ -353,7 +357,10 @@
                     attb[m, pl.ds(q * QP + w * HP, HP), pl.ds(base, 128)] = both[q * HP : q * HP + HP, :]
             return carry
 
-        lax.fori_loop(0, 4, heads, 0)
+        for h in range(2):
+            lax.fori_loop(2 * h, 2 * h + 2, heads, 0, unroll=True)
+            for q in range(4):
+                launch(att_copy, m, q, h)
 
     def block(m, middle, after):
         @pl.when(second)
@@ -361,12 +368,11 @@
             for q in away[m]:
                 halo(m, q, False).wait_recv()
             for q in range(4):
-                att_copy(m, q).wait_recv()
+                for h in range(2):
+                    att_copy(m, q, h).wait_recv()
             add_projected(m, ar, oo, xs)
 
         attend(m, middle)
-        for q in range(4):
-            launch(att_copy, m, q)
         after()
         if m == 0:
             local["o"].wait()
@@ -378,13 +384,13 @@
                 home_copy(m, q).start()
             x2h[m, pl.ds(own[m] * QP, QP), :] = xs[m, pl.ds(own[m] * QP, QP), :]
 
-    def merge(m):
+    def prepare(m):
         def gather(k, carry):
             rows = pl.ds(pl.multiple_of(k * QP, QP), QP)
             jb[k] = jnp.dot(sm[rows, :], x2h[m], preferred_element_type=F32)
             return carry
 
-        lax.fori_loop(0, 4, gather, 0)
+        lax.fori_loop(0, 4, gather, 0, unroll=True)
 
         def ln(n, carry):
             rows = pl.ds(pl.multiple_of(n * 16, 16), 16)
@@ -394,22 +400,25 @@
             var = sum(jnp.sum(p * p, axis=-1, keepdims=True) for p in parts) * (1.0 / 4096)
             scale = lax.rsqrt(var + 1e-05)
             for k in range(4):
-                nb[k, rows, :] = (parts[k] * scale * mg_ref[k]).astype(BF16)
+                nb[k, pl.ds(m * QP + n * 16, 16), :] = (parts[k] * scale * mg_ref[k]).astype(BF16)
             return carry
 
-        lax.fori_loop(0, 5, ln, 0)
-
+        lax.fori_loop(0, 5, ln, 0, unroll=True)
+
+    def project_merged():
         def out(n, carry):
             cols = pl.ds(pl.multiple_of(n * 256, 256), 256)
-            acc = jnp.zeros((QP, 256), F32)
+            acc = jnp.zeros((2 * QP, 256), F32)
             for k in range(4):
                 w = wm[k // 2, pl.ds(4 * (k % 2), 4), :, cols].reshape(1024, 256)
                 acc += jnp.dot(nb[k], w, preferred_element_type=F32)
-            for g in range(18):
-                out_ref[m, g, :, cols] = acc[g * 4 : g * 4 + 4].astype(BF16)
+            for m in range(2):
+                for g in range(18):
+                    row = m * QP + g * 4
+                    out_ref[m, g, :, cols] = acc[row : row + 4].astype(BF16)
             return carry
 
-        lax.fori_loop(0, 4, out, 0)
+        lax.fori_loop(0, 4, out, 0, unroll=True)
 
     lvown[...] = jnp.zeros_like(lvown)
     lvown[0:6, 0:12] = live_ref[...].astype(F32)
@@ -475,12 +484,10 @@
             sends.append((o_side, (n,)))
         for n in range(4):
             sends.append((o_core, (n,)))
-        for u in range(7):
-            for h in range(2):
-                sends.append((side_copy, (u, h)))
-            sends.append((core_copy, (u, 0)))
-        for u in (0, 1, 4, 2, 5):
-            sends.append((core_copy, (u, 1)))
+        for u in range(8):
+            for n in range(2):
+                sends.append((side_copy, (u, n)))
+                sends.append((core_copy, (u, n)))
 
     def both(a, b):
         def run():
@@ -493,21 +500,12 @@
     block(0, both([(w_p1,)], [(w_a, 2)]), both([(w_a, 1), (permute, 1)], [(w_b, 2), (spread2, 1), (spread2, 4)]))
     block(1, both([(w_b, 1)], [(w_a, 3)]), both([(w_a, 2), (o_step1,)], [(w_b, 3), (spread2, 2), (spread2, 5)]))
     only(first, (w_b, 2), (o_step2,), (spread2, 0), (spread2, 1), (spread2, 4), (w_a, 3), (spread2, 2), (spread2, 5), (w_b, 3), (o_step3,))()
-    del pending[:]
-    remake()
-    w_last()
-    for u in (3, 6, 7):
-        spread2(u)
-    local["mw"].wait()
-    local["sm"].wait()
-    for u in range(8):
-        spread3(u)
-
-    for m in range(2):
+    def arrive(m):
         @pl.when(first)
         def _():
             for q in range(4):
-                att_copy(m, q).wait_recv()
+                for h in range(2):
+                    att_copy(m, q, h).wait_recv()
             add_projected(m, ar, oo, x2h)
 
         @pl.when(second)
@@ -515,8 +513,20 @@
             for q in away[m]:
                 home_copy(m, q).wait_recv()
 
-        merge(m)
-
+        prepare(m)
+
+    local["sm"].wait()
+    last = [(w_last,), (spread2, 3), (spread2, 6), (spread2, 7)]
+    only(first, *last)()
+    arrive(0)
+    only(second, *last)()
+    del pending[:]
+    remake()
+    arrive(1)
+    local["mw"].wait()
+    for u in range(8):
+        spread3(u)
+    project_merged()
     for make, args in sends:
         make(*args).wait_send()
 
@@ -562,14 +572,14 @@
             pltpu.VMEM((8, 128), F32),
             pltpu.VMEM((2, 4, 8, 128), F32),
             pltpu.VMEM((4, QP, D), F32),
-            pltpu.VMEM((4, QP, D), BF16),
+            pltpu.VMEM((4, 2 * QP, D), BF16),
             dma((11,)),
-            dma((2, 4)), dma((2, 4)), dma((2, 4)), dma((2, 4)), dma((2, 4)), dma((2, 4)),
+            dma((2, 4, 2)), dma((2, 4, 2)), dma((2, 4)), dma((2, 4)), dma((2, 4)), dma((2, 4)),
             dma((2, 4)), dma((2, 4)), dma((8,)), dma((8,)), dma((2, 2, 4)), dma((2, 2, 4)), dma((1,)), dma((1,)),
             dma((8, 2)), dma((8, 2)), dma((8, 2)), dma((8, 2)),
         ],
         compiler_params=pltpu.CompilerParams(
-            collective_id=0, has_side_effects=True, vmem_limit_bytes=52 * 2**20
+            collective_id=0, has_side_effects=True, vmem_limit_bytes=63 * 2**20
         ),
     )(
         fields.transpose(0, 2, 3, 1, 4).reshape(2, QT, 4, D),

time: 79.2 us -> 65.6 us (0.83)
  local copies, waits for them, and re-layouts: 8.33 us -> 1.79 us
  Pallas kernels: 70 us -> 63.6 us
    unnamed x19 -> x1, local copies, waits for them, and re-layouts: 8.33 us -> 1.79 us
    pallas_call x1, Pallas kernels: 70 us -> 63.6 us  [body(): pl.pallas_call(kernel, out_shape=jax.ShapeDtypeStruct((2, 18, 4, 1024), B...]
where the time goes in v2:
time: 65.6 us; the launch traced here: 65.4 us
  Pallas kernels  63.6 us (97%)
  local copies, waits for them, and re-layouts  1.79 us (3%)
    pallas_call x1, Pallas kernels, body(): pl.pallas_call(kernel, out_shape=jax.ShapeDtypeStruct((2, 18, 4, 1024), B...  63.6 us
    unnamed x1, local copies, waits for them, and re-layouts  1.79 us

profile of v2, /device:TPU:5, one launch (start us, length us, event | category | flops | bytes accessed | tf_op | source)
XLA Modules:
  0.0 65.4 jit_solution(8895115439438983425)
XLA Ops:
  0.0 63.6 %shard_map.136 = bf16[2,18,4,1024]{3,2,1,0:T(4,128)(2,1)} custom-call(bf16[2,72,4,1024]{3,2,1,0:T(4,128)(2,1)} %bitcast.11, s32[6,12]{1,0:T(8,128)} %live_ref.1, bf16[1,1024]{1,0:T(2,128)(2,1)} %ng_ref.1, bf16[1024,512]{1,0:T(8,128)(2,1)} %bitcast.13, bf16[1024,512]{1,0:T(8,128)(2,1)} %bitcast.14, bf16[1024,512]{1,0:T(8,128)(2,1)} %bitcast.15, ...), custom_call_target="tpu_custom_call" | custom-call | tf_op jit(solution)/shard_map/pallas_call | solution.py:547
  63.6 1.8 %copy.16 = bf16[2,4,3,6,1024]{4,1,3,2,0:T(4,128)(2,1)} copy(bf16[2,4,3,6,1024]{4,1,3,2,0:T(4,128)(2,1)} %bitcast.12) | data formatting | bytes 589824

commit v3 on v2

--- a/solution.py
+++ b/solution.py
@@ -245,7 +245,7 @@
         return (1 - q // 2, 1 - q % 2) if m == 0 else (-(q // 2), -(q % 2))
 
     own = (3, 0)
-    away = ((0, 1, 2), (1, 2, 3))
+    away = ((0, 1, 2), (3, 2, 1))
 
     def permute(m):
         local[f"x{m}"].wait()
@@ -359,7 +359,7 @@
 
         for h in range(2):
             lax.fori_loop(2 * h, 2 * h + 2, heads, 0, unroll=True)
-            for q in range(4):
+            for q in (range(4), range(3, -1, -1))[m]:
                 launch(att_copy, m, q, h)
 
     def block(m, middle, after):

time: 65.6 us -> 65.5 us (level)
  no operation moved by 1% of the time
where the time goes in v3:
time: 65.5 us; the launch traced here: 65.3 us
  Pallas kernels  63.5 us (97%)
  local copies, waits for them, and re-layouts  1.79 us (3%)
    pallas_call x1, Pallas kernels, body(): pl.pallas_call(kernel, out_shape=jax.ShapeDtypeStruct((2, 18, 4, 1024), B...  63.5 us
    unnamed x1, local copies, waits for them, and re-layouts  1.79 us

profile of v3, /device:TPU:5, one launch (start us, length us, event | category | flops | bytes accessed | tf_op | source)
XLA Modules:
  0.0 65.3 jit_solution(2157250995333992289)
XLA Ops:
  0.0 63.5 %shard_map.136 = bf16[2,18,4,1024]{3,2,1,0:T(4,128)(2,1)} custom-call(bf16[2,72,4,1024]{3,2,1,0:T(4,128)(2,1)} %bitcast.11, s32[6,12]{1,0:T(8,128)} %live_ref.1, bf16[1,1024]{1,0:T(2,128)(2,1)} %ng_ref.1, bf16[1024,512]{1,0:T(8,128)(2,1)} %bitcast.13, bf16[1024,512]{1,0:T(8,128)(2,1)} %bitcast.14, bf16[1024,512]{1,0:T(8,128)(2,1)} %bitcast.15, ...), custom_call_target="tpu_custom_call" | custom-call | tf_op jit(solution)/shard_map/pallas_call | solution.py:547
  63.5 1.8 %copy.16 = bf16[2,4,3,6,1024]{4,1,3,2,0:T(4,128)(2,1)} copy(bf16[2,4,3,6,1024]{4,1,3,2,0:T(4,128)(2,1)} %bitcast.12) | data formatting | bytes 589824
